TPU v7x, 32 devices: a whole 2x2x4 slice. The times are simulated.
32 devices in a mesh: layer: 2 (over core), ex: 16 (over z, y, x).
Axes of the slice: x: 2, y: 2, z: 4, core: 2. Of those that a mesh axis runs over, the one named last changes fastest.
Arguments:
- train_sketch: bfloat16 [12, 8192, 256], P('layer', 'ex')
- val_sketch: bfloat16 [12, 512, 256], P('layer', 'ex')
- first_moment: float32 [12, 256], P('layer'), may hold values from -0.6 to 0.6
- second_moment: float32 [12, 256], P('layer'), may hold values from 0.01 to 1
- train_pair: int32 [8192], P('ex'), may hold values from 0 to 15
- val_pair: int32 [512], P('ex'), may hold values from 0 to 15
- block_mask: int32 [16, 16], replicated, may hold values 0 or 1
Outputs:
- scores: bfloat16 [4096, 2, 512], P('ex', 'layer')
All inputs are finite; a program needn't handle non-finite values.
Results may differ from a plain program's by a relative error of at most 0.0058.
Values may be sent and summed in bfloat16 or wider, within the bound.
A program may use at most 128 MiB of HBM per device.

v0:
```python
import jax
import jax.numpy as jnp
from jax import lax
from jax.sharding import PartitionSpec as P


def precondition(grad, first_moment, second_moment):
    return (0.9 * first_moment[:, None, :] + 0.1 * grad) / (
        jnp.sqrt(0.999 * second_moment[:, None, :] + 0.001 * grad * grad) + 1e-08
    )


def squares(values):
    return jnp.sum(values * values, axis=(0, 2))


def unit_rows(values, total_sq, scale_factor):
    return (values * (scale_factor * lax.rsqrt(total_sq + 1e-06))[None, :, None]).astype(
        jnp.bfloat16
    )


def contract(left, right):
    return lax.dot_general(
        left, right, (((0, 2), (0, 2)), ((), ())), preferred_element_type=jnp.float32
    )


def local(train_sketch, val_sketch, first_moment, second_moment, train_pair, val_pair, block_mask):
    lay_dev, tr_ex, width = train_sketch.shape
    layer_count = lax.axis_size("layer")
    rows_here = tr_ex // layer_count
    scale_factor = float(lay_dev * layer_count * width) ** 0.25
    pair_count = block_mask.shape[0]
    labels = jnp.arange(pair_count, dtype=jnp.int32)
    val_all = lax.all_gather(val_sketch, "ex", axis=1, tiled=True)
    val_labels = lax.all_gather(val_pair, "ex", axis=0, tiled=True)
    val_onehot = (labels[:, None] == val_labels[None, :]).astype(jnp.bfloat16)
    pairs_here = lax.dynamic_slice_in_dim(
        train_pair, lax.axis_index("layer") * rows_here, rows_here, 0
    )
    mine = lax.all_to_all(train_sketch, "layer", split_axis=1, concat_axis=0, tiled=True)
    first_all, second_all = (
        lax.all_gather(first_moment, "layer", axis=0, tiled=True),
        lax.all_gather(second_moment, "layer", axis=0, tiled=True),
    )
    val_full = lax.all_gather(val_all, "layer", axis=0, tiled=True)
    pre = precondition(mine.astype(jnp.float32), first_all, second_all)
    unit_train = unit_rows(pre, squares(pre), scale_factor)
    val_float = val_full.astype(jnp.float32)
    unit_val = unit_rows(val_float, squares(val_float), scale_factor)
    raw = contract(unit_train, unit_val)
    train_onehot = (pairs_here[:, None] == labels[None, :]).astype(jnp.bfloat16)
    row_mask = jnp.dot(
        train_onehot, block_mask.astype(jnp.bfloat16), preferred_element_type=jnp.float32
    ).astype(jnp.bfloat16)
    weights = jnp.dot(row_mask, val_onehot, preferred_element_type=jnp.float32)
    return (raw * weights).astype(jnp.bfloat16)[:, None, :]


def solution(mesh):
    placed = (
        P("layer", "ex", None),
        P("layer", "ex", None),
        P("layer", None),
        P("layer", None),
        P("ex"),
        P("ex"),
        P(),
    )
    return jax.shard_map(
        local, mesh=mesh, in_specs=placed, out_specs=P("ex", "layer", None), check_vma=False
    )
```

profile of v0, /device:TPU:0, one launch (start us, length us, event | category | flops | bytes accessed | tf_op | source)
XLA Modules:
  0.0 121.1 jit_solution(10765532577256059378)
XLA Ops:
  6.5 0.0 all-gather.5.cloned.1.call-start
  6.5 0.7 all-gather.5.cloned.1.call-update
  7.3 0.0 all-gather.7.cloned.1.call-start
  7.3 63.5 %all-gather.5.cloned.1.call-done = bf16[6,512,256]{2,1,0:T(8,128)(2,1)} async-done(((bf16[6,32,256]{2,1,0:T(8,128)(2,1)}), bf16[6,512,256]{2,1,0:T(8,128)(2,1)}) %all-gather.5.cloned.1.call-update) | async-done | bytes 1572880 | tf_op jit(solution)/shard_map/all_gather | solution.py:36
  70.8 0.0 all-gather.7.cloned.1.call-update
  70.8 3.7 %copy.14 = bf16[6,512,256]{2,0,1:T(8,128)(2,1)} copy(bf16[6,512,256]{2,1,0:T(8,128)(2,1)} %param.7) | data formatting | bytes 3145728 | tf_op args[0]
  74.5 3.9 %all-to-all-start = ((bf16[6,512,256]{2,0,1:T(8,128)(2,1)}), bf16[6,512,256]{2,0,1:T(8,128)(2,1)S(1)}, u32[]{:S(2)}, u32[]{:S(2)}) async-start(bf16[6,512,256]{2,0,1:T(8,128)(2,1)} %copy.14), calls=%async_computation | async-start | bytes 4194304 | tf_op jit(solution)/shard_map/all_to_all | solution.py:42
  78.4 2.8 %all-to-all-done = bf16[6,512,256]{2,0,1:T(8,128)(2,1)S(1)} async-done(((bf16[6,512,256]{2,0,1:T(8,128)(2,1)}), bf16[6,512,256]{2,0,1:T(8,128)(2,1)S(1)}, u32[]{:S(2)}, u32[]{:S(2)}) %all-to-all-start) | async-done | bytes 1572896 | tf_op jit(solution)/shard_map/all_to_all | solution.py:42
  81.2 0.3 convert_bitcast_fusion
  81.6 0.0 copy-start.2
  81.6 0.0 copy-start.3
  81.6 0.0 copy-start.4
  81.6 0.0 copy-start.6
  81.6 0.0 copy-start.5
  81.6 2.6 %copy.15 = f32[2,6,256,256]{3,2,1,0:T(8,128)} copy(f32[2,6,256,256]{3,1,2,0:T(8,128)S(1)} %convert_bitcast_fusion) | data formatting | bytes 6291456 | tf_op jit(solution)/shard_map/convert_element_type | solution.py:48
  84.2 0.0 copy-done.2
  84.2 1.8 %all-gather = f32[2,6,256]{2,1,0:T(8,128)S(1)} all-gather(f32[1,6,256]{2,1,0:T(8,128)S(1)} %bitcast.25), channel_id=1, replica_groups=mesh['layer'=2,'ex'=16] {'layer'}, dimensions={0}, use_global_device_ids=true | all-gather | bytes 18432 | tf_op jit(solution)/shard_map/all_gather | solution.py:44
  86.1 0.0 copy-done.3
  86.1 1.8 %all-gather.1 = f32[2,6,256]{2,1,0:T(8,128)S(1)} all-gather(f32[1,6,256]{2,1,0:T(8,128)S(1)} %bitcast.26), channel_id=1, replica_groups=mesh['layer'=2,'ex'=16] {'layer'}, dimensions={0}, use_global_device_ids=true | all-gather | bytes 18432 | tf_op jit(solution)/shard_map/all_gather | solution.py:45
  87.9 0.0 copy-done.4
  87.9 0.1 dynamic_slice.3
  88.0 0.0 copy-done.6
  88.0 0.6 dynamic-slice
  89.2 0.0 copy-done.5
  89.2 0.2 dynamic-update-slice
  89.5 13.1 %all-reduce = s32[512]{0:T(512)S(1)} all-reduce(s32[512]{0:T(512)S(1)} %dynamic-update-slice), channel_id=1, replica_groups=mesh['layer'=2,'ex'=16] {'ex'}, use_global_device_ids=true, to_apply=%add | all-reduce | flops 512 | bytes 4096
  102.6 2.9 %fusion.7 = f32[256]{0:T(256)S(1)} fusion(f32[2,6,256]{2,1,0:T(8,128)S(1)} %broadcast_multiply_fusion, f32[2,6,256]{2,1,0:T(8,128)S(1)} %broadcast_multiply_fusion.1, bf16[6,2,256,256]{3,0,2,1:T(8,128)(2,1)S(1)} %bitcast.24), kind=kLoop, calls=%fused_computation.12 | loop fusion | flops 7864064 | bytes 1598464 | tf_op jit(solution)/shard_map/reduce_sum | solution.py:14
  105.5 3.6 %fusion.17 = bf16[12,256,256]{2,1,0:T(8,128)(2,1)S(1)} fusion(f32[2,6,256,256]{3,2,1,0:T(8,128)} %copy.15, f32[256]{0:T(256)S(1)} %rsqrt_multiply_fusion.1, f32[12,256]{1,0:T(8,128)S(1)} %reshape.37, f32[12,256]{1,0:T(8,128)S(1)} %reshape.35), kind=kLoop, calls=%fused_computation.22 | loop fusion | flops 7077888 | bytes 4744192 | tf_op jit(solution)/shard_map/convert_element_type | solution.py:18
  109.1 0.0 all-gather.7.cloned.1.call-done
  109.1 0.0 copy-start
  109.1 2.7 %fusion = f32[512]{0:T(512)S(1)} fusion(bf16[12,512,256]{2,1,0:T(8,128)(2,1)} %all-gather.7.cloned.1.call-done), kind=kLoop, calls=%fused_computation.2 | loop fusion | flops 4718080 | bytes 3147776 | tf_op jit(solution)/shard_map/reduce_sum | solution.py:14
  111.9 0.1 copy-done
  111.9 0.0 copy-start.1
  111.9 1.1 fusion.18
  113.1 0.0 copy-done.1
  113.1 1.2 fusion.22
  (7 shorter events, 0.0 us)
Async XLA Ops:
  6.5 64.3 %all-gather.5.cloned.1.call-start = ((), (), s32[]{:S(2)}) async-start(), calls=%async_computation.1 | async-start | bytes 1671168 | tf_op jit(solution)/shard_map/all_gather | solution.py:36
  7.3 101.8 %all-gather.7.cloned.1.call-start = ((), (), s32[]{:S(2)}) async-start(), calls=%async_computation.2 | async-start | bytes 4718592 | tf_op jit(solution)/shard_map/all_gather | solution.py:47
  74.5 6.7 %all-to-all-start = ((bf16[6,512,256]{2,0,1:T(8,128)(2,1)}), bf16[6,512,256]{2,0,1:T(8,128)(2,1)S(1)}, u32[]{:S(2)}, u32[]{:S(2)}) async-start(bf16[6,512,256]{2,0,1:T(8,128)(2,1)} %copy.14), calls=%async_computation | async-start | bytes 4194304 | tf_op jit(solution)/shard_map/all_to_all | solution.py:42
  81.6 2.7 %copy-start.2 = (f32[6,256]{1,0:T(8,128)S(1)}, f32[6,256]{1,0:T(8,128)}, u32[]{:S(2)}) copy-start(f32[6,256]{1,0:T(8,128)} %param.9) | copy-start | bytes 18436
  81.6 4.5 %copy-start.3 = (f32[6,256]{1,0:T(8,128)S(1)}, f32[6,256]{1,0:T(8,128)}, u32[]{:S(2)}) copy-start(f32[6,256]{1,0:T(8,128)} %param.10) | copy-start | bytes 18436
  81.6 6.3 %copy-start.4 = (s32[512]{0:T(512)S(1)}, s32[512]{0:T(512)}, u32[]{:S(2)}) copy-start(s32[512]{0:T(512)} %param.11) | copy-start | bytes 6148
  81.6 6.4 %copy-start.6 = (u32[32]{0:T(128)S(1)}, u32[32]{0:T(128)}, u32[]{:S(2)}) copy-start(u32[32]{0:T(128)} %constant.32) | copy-start | bytes 388
  81.6 7.6 %copy-start.5 = (s32[32]{0:T(128)S(1)}, s32[32]{0:T(128)}, u32[]{:S(2)}) copy-start(s32[32]{0:T(128)} %param.12) | copy-start | bytes 388
  109.1 2.8 %copy-start = (bf16[12,512,256]{2,1,0:T(8,128)(2,1)S(1)}, bf16[12,512,256]{2,1,0:T(8,128)(2,1)}, u32[]{:S(2)}) copy-start(bf16[12,512,256]{2,1,0:T(8,128)(2,1)} %all-gather.7.cloned.1.call-done) | copy-start | bytes 9437188
  111.9 1.1 copy-start.1
Sparse Core Ops, SparseCore 0:
  10.1 60.6 all-gather.4
  72.3 11.0 all-gather.6
where the time goes:
time: 121 us
  waiting for transfers between devices  67.1 us (55%)
  blocking collectives  16.7 us (14%)
  between operations  14.2 us (12%)
  other arithmetic  9.57 us (8%)
  local copies, waits for them, and re-layouts  7.33 us (6%)
  starting transfers between devices  3.92 us (3%)
  matrix products  2.33 us (2%)
    all_gather x1, waiting for transfers between devices, local(): val_all = lax.all_gather(val_sketch, 'ex', axis=1, tiled=True)  63.5 us
    unnamed x1, blocking collectives  13.1 us
    reduce_sum x2, other arithmetic, squares(): return jnp.sum(values * values, axis=(0, 2))  5.64 us
    unnamed x18, local copies, waits for them, and re-layouts  4.62 us
    all_to_all x1, starting transfers between devices, local(): lax.all_to_all(train_sketch, 'layer', split_axis=1, concat_axis=0, tiled=...  3.88 us
    convert_element_type x1, other arithmetic, unit_rows(): (values * (scale_factor * lax.rsqrt(total_sq + 1e-06))[None, :, None]).as...  3.58 us
    all_to_all x1, waiting for transfers between devices, local(): lax.all_to_all(train_sketch, 'layer', split_axis=1, concat_axis=0, tiled=...  2.84 us
    convert_element_type x1, local copies, waits for them, and re-layouts, local(): pre = precondition(mine.astype(jnp.float32), first_all, second_all)  2.62 us
  transfers between devices with their start and end apart: 3, of which 2 were waited for; matrix products, arithmetic and copies ran while one was open for 12% of the time, Pallas kernels for 0%

commit v1 on v0

v1 whole, which is shorter than its diff:
```python
import functools

import jax
import jax.numpy as jnp
from jax import lax
from jax.experimental import pallas as pl
from jax.experimental.pallas import tpu as pltpu
from jax.sharding import PartitionSpec as P

MESH = pl.DeviceIdType.MESH
LANES = 128
CHUNK = 32


def box_of(count):
    side = 1
    while (side * 2) ** 3 * 2 <= count and count % ((side * 2) ** 2) == 0:
        side *= 2
    return count // (side * side), side, side


def visit(here, extent, step):
    if step == 0:
        return here
    below, above = here, extent - 1 - here
    least = jnp.minimum(below, above)
    near = here - (step + 1) // 2 if step % 2 else here + step // 2
    far = jnp.where(below < above, here + (step - least), here - (step - least))
    return jnp.where(step <= 2 * least, near, far)


class Sends:
    def __init__(self, sems):
        self.sems = sems
        self.made = []

    def go(self, src, dst, recv_sem, target, cond=None):
        index = len(self.made)

        def make():
            return pltpu.make_async_remote_copy(
                src_ref=src,
                dst_ref=dst,
                send_sem=self.sems.at[index],
                recv_sem=recv_sem,
                device_id=target,
                device_id_type=MESH,
            )

        self.made.append((make, cond))
        if cond is None:
            make().start()
        else:
            pl.when(cond)(lambda: make().start())

    def finish(self):
        for make, cond in self.made:
            if cond is None:
                make().wait_send()
            else:
                pl.when(cond)(lambda make=make: make().wait_send())


def send_sites(box, planes):
    z_n, y_n, x_n = box
    line = lambda n: 0 if n == 1 else 1 if n == 2 else 2 + (n - 1)
    per = 2 + 2 * (line(y_n) + line(x_n) + y_n * line(x_n) + x_n * line(y_n))
    return z_n * (per + 4) + 16 + 2 * z_n + 3 * (z_n + y_n + x_n)


def kernel(
    box, scale_factor,
    train_hbm, val_hbm, first_ref, second_ref, tpair_ref, vpair_ref, mask_ref,
    out_ref,
    gath, train, pre, tsq, tsq_in, part_out, part_in, own_part, vsq, vsq_in, labels,
    local_sems, send_sems, block_sems, pair_sems, label_sems,
):
    z_n, y_n, x_n = box
    plane_blocks = y_n * x_n
    lay_dev, tr_ex, width = train.shape
    val_dev = gath.shape[2]
    half = lay_dev // 2
    rows = out_ref.shape[0]
    tile_blocks = LANES // val_dev
    tiles = plane_blocks // tile_blocks
    pair_count = mask_ref.shape[0]
    core = lax.axis_index("layer")
    me = lax.axis_index("ex")
    z, y, x = me // plane_blocks, (me // x_n) % y_n, me % x_n
    slot = lambda a, b, c: (a * y_n + b) * x_n + c
    at_ex = lambda a, b, c: {"ex": slot(a, b, c)}
    other_core = {"layer": 1 - core}
    sends = Sends(send_sems)

    train_copy = pltpu.make_async_copy(train_hbm, train, local_sems.at[0])
    train_copy.start()
    val_copy = pltpu.make_async_copy(val_hbm, gath.at[me], local_sems.at[1])
    val_copy.start()

    def neighbours(dim):
        here, extent = ((z, z_n), (y, y_n), (x, x_n))[dim]

        def device(pos):
            return at_ex(*(pos if d == dim else c for d, c in enumerate((z, y, x))))

        if extent == 1:
            return []
        if extent == 2:
            return [(device(1 - here), None)]
        return [(device(here + 1), here < extent - 1), (device(here - 1), here > 0)]

    def onward(dim, came_from):
        here, extent = ((z, z_n), (y, y_n), (x, x_n))[dim]
        if extent <= 2:
            return []
        pos = jnp.where(came_from < here, here + 1, here - 1)
        device = at_ex(*(pos if d == dim else c for d, c in enumerate((z, y, x))))
        return [(device, jnp.logical_and(pos >= 0, pos < extent))]

    barrier = pltpu.get_barrier_semaphore()
    pl.semaphore_signal(barrier, inc=1, device_id=other_core, device_id_type=MESH)
    expected = 1
    for dim in range(3):
        for device, cond in neighbours(dim):
            def greet(device=device):
                pl.semaphore_signal(barrier, inc=1, device_id=device, device_id_type=MESH)

            if cond is None:
                greet()
                expected = expected + 1
            else:
                pl.when(cond)(greet)
                expected = expected + jnp.where(cond, 1, 0)
    pl.semaphore_wait(barrier, expected)

    def block(h, where):
        return gath.at[where, pl.ds(h * half, half)]

    def send_block(h, where, targets, own=False):
        src = val_hbm.at[pl.ds(h * half, half)] if own else block(h, where)
        for device, cond in targets:
            sends.go(src, block(h, where), block_sems.at[h, where], device, cond)

    def wait_block(h, where):
        pltpu.make_async_copy(block(h, where), block(h, where), block_sems.at[h, where]).wait()

    order = ((1, 2), (2, 1))

    def column(step):
        plane = visit(z, z_n, step)
        where = slot(plane, y, x)
        for h in (0, 1):
            if step:
                wait_block(h, where)
                send_block(h, where, onward(0, plane))
            else:
                send_block(h, where, neighbours(0), True)
            send_block(h, where, neighbours(order[h][0]), not step)
        for h in (0, 1):
            send_block(h, where, neighbours(order[h][1]), not step)

    def second(step):
        plane = visit(z, z_n, step)
        for h in (0, 1):
            dim, last = order[h]
            here, extent = ((z, z_n), (y, y_n), (x, x_n))[dim]
            for k in range(1, extent):
                pos = visit(here, extent, k)
                where = slot(plane, pos, x) if dim == 1 else slot(plane, y, pos)
                wait_block(h, where)
                send_block(h, where, onward(dim, pos))
                send_block(h, where, neighbours(last))

    def third(step):
        plane = visit(z, z_n, step)
        for h in (0, 1):
            dim, last = order[h]
            here, extent = ((z, z_n), (y, y_n), (x, x_n))[dim]
            here_last, extent_last = ((z, z_n), (y, y_n), (x, x_n))[last]
            for k in range(extent):
                pos = visit(here, extent, k)
                for m in range(1, extent_last):
                    end = visit(here_last, extent_last, m)
                    where = slot(plane, pos, end) if dim == 1 else slot(plane, end, pos)
                    wait_block(h, where)
                    send_block(h, where, onward(last, end))

    def label_group(dim, pos):
        if dim == 2:
            return labels.at[pl.ds(slot(z, y, pos), 1)]
        if dim == 1:
            return labels.at[pl.ds(slot(z, pos, 0), x_n)]
        return labels.at[pl.ds(slot(pos, 0, 0), plane_blocks)]

    def send_labels(dim, pos, targets):
        for device, cond in targets:
            sends.go(
                label_group(dim, pos), label_group(dim, pos), label_sems.at[dim, pos], device, cond
            )

    def label_start(dim):
        send_labels(dim, (z, y, x)[dim], neighbours(dim))

    def label_take(dim, step):
        here, extent = ((z, z_n), (y, y_n), (x, x_n))[dim]
        pos = visit(here, extent, step)
        group = label_group(dim, pos)
        pltpu.make_async_copy(group, group, label_sems.at[dim, pos]).wait()
        send_labels(dim, pos, onward(dim, pos))

    def label_line(dim):
        for k in range(1, (z_n, y_n, x_n)[dim]):
            label_take(dim, k)

    def precondition(start, stop):
        @pl.loop(start // CHUNK, stop // CHUNK)
        def _(c):
            here = pl.ds(pl.multiple_of(c * CHUNK, CHUNK), CHUNK)
            total = jnp.zeros((CHUNK, width), jnp.float32)
            for l in range(lay_dev):
                grad = train[l, here, :].astype(jnp.float32)
                first = first_ref[pl.ds(l, 1), :] * 0.9
                second_m = second_ref[pl.ds(l, 1), :] * 0.999
                root = lax.rsqrt(second_m + 0.001 * grad * grad)
                value = (first + 0.1 * grad) * root / (1.0 + 1e-08 * root)
                total = total + value * value
                pre[l, here, :] = value.astype(jnp.bfloat16)
            tsq[here, :] = jnp.broadcast_to(jnp.sum(total, axis=1, keepdims=True), (CHUNK, LANES))

    mine = pl.ds(pl.multiple_of(core * rows, rows), rows)
    theirs = pl.ds(pl.multiple_of((1 - core) * rows, rows), rows)

    def product(step):
        plane = visit(z, z_n, step)
        for j in range(tiles):
            cols = pl.ds(j * LANES, LANES)
            blocks = pl.ds(plane * plane_blocks + j * tile_blocks, tile_blocks)
            layer = lambda l: gath[blocks, l].reshape(LANES, width)

            def dot(where):
                total = None
                for l in range(lay_dev):
                    term = lax.dot_general(
                        pre[l, where, :], layer(l), (((1,), (1,)), ((), ())),
                        preferred_element_type=jnp.float32,
                    )
                    total = term if total is None else total + term
                return total

            part_out[step, :, cols] = dot(theirs).astype(jnp.bfloat16)
            if j == tiles - 1:
                sends.go(part_out.at[step], part_in.at[step], pair_sems.at[0, step], other_core)
            squares = None
            for l in range(lay_dev):
                value = layer(l).astype(jnp.float32)
                squares = value * value if squares is None else squares + value * value
            vsq[step, :, cols] = lax.dot_general(
                jnp.ones((8, width), jnp.float32), squares, (((1,), (1,)), ((), ())),
                precision=lax.Precision.HIGHEST, preferred_element_type=jnp.float32,
            )
            if j == tiles - 1:
                sends.go(vsq.at[step], vsq_in.at[step], pair_sems.at[1, step], other_core)
            own_part[step, :, cols] = dot(mine)

    def pair_wait(buffer, sem):
        pltpu.make_async_copy(buffer, buffer, sem).wait()

    def finish(step):
        plane = visit(z, z_n, step)
        pair_ids = lax.broadcasted_iota(jnp.int32, (pair_count, rows), 0)
        row_hot = (pair_ids == tpair_ref[:, mine]).astype(jnp.float32).astype(jnp.bfloat16)
        table = mask_ref[...].astype(jnp.float32).astype(jnp.bfloat16)
        label_ids = lax.broadcasted_iota(jnp.int32, (pair_count, LANES), 0)
        row_scale = (scale_factor * scale_factor) * lax.rsqrt(tsq[mine, :] + tsq_in[...] + 1e-06)
        weights = []
        for j in range(tiles):
            first = plane * plane_blocks + j * tile_blocks
            row = labels[first]
            for i in range(1, tile_blocks):
                row = jnp.maximum(row, labels[first + i])
            val_hot = (label_ids == row).astype(jnp.float32).astype(jnp.bfloat16)
            val_table = jnp.dot(table, val_hot, preferred_element_type=jnp.float32)
            weights.append(
                row_scale
                * lax.dot_general(
                    row_hot, val_table.astype(jnp.bfloat16), (((0,), (0,)), ((), ())),
                    preferred_element_type=jnp.float32,
                )
            )
        pair_wait(vsq_in.at[step], pair_sems.at[1, step])
        pair_wait(part_in.at[step], pair_sems.at[0, step])
        for j in range(tiles):
            cols = pl.ds(j * LANES, LANES)
            total_sq = vsq[step, pl.ds(0, 1), cols] + vsq_in[step, pl.ds(0, 1), cols]
            weight = weights[j] * lax.rsqrt(total_sq + 1e-06)
            raw = own_part[step, :, cols] + part_in[step, :, cols].astype(jnp.float32)
            place = pl.multiple_of((plane * tiles + j) * LANES, LANES)
            out_ref[:, pl.ds(place, LANES)] = jnp.where(weight != 0.0, raw * weight, 0.0).astype(
                jnp.bfloat16
            )

    column(0)
    lane_block = lax.broadcasted_iota(jnp.int32, (1, LANES), 1) // val_dev
    own_labels = jnp.concatenate([vpair_ref[...]] * tile_blocks, axis=1)
    labels[me] = jnp.where(lane_block == me % tile_blocks, own_labels, -1)
    label_start(2)
    train_copy.wait()
    precondition(0, tr_ex // 2)
    label_line(2)
    label_start(1)
    second(0)
    for step in range(1, z_n):
        column(step)
        if step == 1:
            precondition(tr_ex // 2, tr_ex)
            sends.go(tsq.at[theirs], tsq_in, local_sems.at[2], other_core)
            label_line(1)
            label_start(0)
            second(step)
            val_copy.wait()
        else:
            label_take(0, step - 1)
            third(step - 2)
            product(step - 2)
            second(step)
    pair_wait(tsq_in, local_sems.at[2])
    if z_n > 1:
        label_take(0, z_n - 1)
        third(z_n - 2)
        product(z_n - 2)
    for step in range(z_n - 2):
        finish(step)
    third(z_n - 1)
    product(z_n - 1)
    for step in range(max(z_n - 2, 0), z_n):
        finish(step)
    sends.finish()


def solution(mesh):
    box = box_of(mesh.shape["ex"])

    def local(
        train_sketch, val_sketch, first_moment, second_moment, train_pair, val_pair, block_mask
    ):
        lay_dev, tr_ex, width = train_sketch.shape
        val_dev = val_sketch.shape[1]
        ex_n, layer_n = mesh.shape["ex"], mesh.shape["layer"]
        rows = tr_ex // layer_n
        z_n, y_n, x_n = box
        plane_cols = y_n * x_n * val_dev
        scale_factor = float(lay_dev * layer_n * width) ** 0.25
        vmem = pl.BlockSpec(memory_space=pltpu.VMEM)
        hbm = pl.BlockSpec(memory_space=pl.ANY)
        scores = pl.pallas_call(
            functools.partial(kernel, box, scale_factor),
            out_shape=jax.ShapeDtypeStruct((rows, ex_n * val_dev), jnp.bfloat16),
            in_specs=[hbm, hbm, vmem, vmem, vmem, vmem, vmem],
            out_specs=vmem,
            scratch_shapes=[
                pltpu.VMEM((ex_n, lay_dev, val_dev, width), jnp.bfloat16),
                pltpu.VMEM((lay_dev, tr_ex, width), jnp.bfloat16),
                pltpu.VMEM((lay_dev, tr_ex, width), jnp.bfloat16),
                pltpu.VMEM((tr_ex, LANES), jnp.float32),
                pltpu.VMEM((rows, LANES), jnp.float32),
                pltpu.VMEM((z_n, rows, plane_cols), jnp.bfloat16),
                pltpu.VMEM((z_n, rows, plane_cols), jnp.bfloat16),
                pltpu.VMEM((z_n, rows, plane_cols), jnp.float32),
                pltpu.VMEM((z_n, 8, plane_cols), jnp.float32),
                pltpu.VMEM((z_n, 8, plane_cols), jnp.float32),
                pltpu.VMEM((ex_n, 1, LANES), jnp.int32),
                pltpu.SemaphoreType.DMA((3,)),
                pltpu.SemaphoreType.DMA((send_sites(box, z_n),)),
                pltpu.SemaphoreType.DMA((2, ex_n)),
                pltpu.SemaphoreType.DMA((2, z_n)),
                pltpu.SemaphoreType.DMA((3, max(box))),
            ],
            compiler_params=pltpu.CompilerParams(
                collective_id=0, has_side_effects=True, vmem_limit_bytes=48 * 1024 * 1024
            ),
        )(
            train_sketch, val_sketch, first_moment, second_moment,
            train_pair[None, :], val_pair[None, :], block_mask,
        )
        return scores[:, None, :]

    placed = (
        P("layer", "ex", None),
        P("layer", "ex", None),
        P("layer", None),
        P("layer", None),
        P("ex"),
        P("ex"),
        P(),
    )
    return jax.shard_map(
        local, mesh=mesh, in_specs=placed, out_specs=P("ex", "layer", None), check_vma=False
    )
```

time: 121 us -> 36.5 us (0.30)
  waiting for transfers between devices: 67.1 us -> 0 us
  Pallas kernels: 0 us -> 29.7 us
  blocking collectives: 16.7 us -> 0 us
  between operations: 14.2 us -> 0.02 us
  other arithmetic: 9.57 us -> 0 us
  starting transfers between devices: 3.92 us -> 0 us
  matrix products: 2.33 us -> 0 us
    all_gather x2 -> x0, waiting for transfers between devices: 63.5 us -> none  [the longest x1 63.5 us: local(): val_all = lax.all_gather(val_sketch, 'ex', axis=1, tiled=True)]
    pallas_call x0 -> x1, Pallas kernels: none -> 29.7 us  [local(): pl.pallas_call(functools.partial(kernel, box, scale_factor), out_shape=ja...]
    unnamed x1 -> x0, blocking collectives: 13.1 us -> none
    reduce_sum x2 -> x0, other arithmetic: 5.64 us -> none  [squares(): return jnp.sum(values * values, axis=(0, 2))]
    convert_element_type x2 -> x0, other arithmetic: 3.91 us -> none  [the longest x1 3.58 us: unit_rows(): (values * (scale_factor * lax.rsqrt(total_sq + 1e-06))[None, :, None]).as...]
    all_to_all x1 -> x0, starting transfers between devices: 3.88 us -> none  [local(): lax.all_to_all(train_sketch, 'layer', split_axis=1, concat_axis=0, tiled=...]
    all_gather x2 -> x0, blocking collectives: 3.61 us -> none  [the longest x1 1.81 us: local(): lax.all_gather(second_moment, 'layer', axis=0, tiled=True)]
    all_to_all x1 -> x0, waiting for transfers between devices: 2.84 us -> none  [local(): lax.all_to_all(train_sketch, 'layer', split_axis=1, concat_axis=0, tiled=...]
  transfers between devices with their start and end apart: 3 -> 0, of which waited for: 2 -> 0; matrix products, arithmetic and copies ran while one was open for 12% -> 0% of each run, Pallas kernels for 0% -> 0%
where the time goes in v1:
time: 36.5 us; the launch traced here: 36.1 us
  Pallas kernels  29.7 us (81%)
  local copies, waits for them, and re-layouts  6.43 us (18%)
    pallas_call x1, Pallas kernels, local(): pl.pallas_call(functools.partial(kernel, box, scale_factor), out_shape=ja...  29.7 us
    unnamed x15, local copies, waits for them, and re-layouts  6.43 us

profile of v1, /device:TPU:0, one launch (start us, length us, event | category | flops | bytes accessed | tf_op | source)
XLA Modules:
  0.0 36.1 jit_solution(2088994910894197136)
XLA Ops:
  0.0 0.0 copy-start
  0.0 1.4 %copy-done = bf16[6,512,256]{2,1,0:T(8,128)(2,1)S(1)} copy-done((bf16[6,512,256]{2,1,0:T(8,128)(2,1)S(1)}, bf16[6,512,256]{2,1,0:T(8,128)(2,1)}, u32[]{:S(2)}) %copy-start) | copy-done | bytes 1572888
  1.4 0.0 copy-start.1
  1.4 0.9 %copy-done.1 = bf16[6,32,256]{2,1,0:T(8,128)(2,1)S(1)} copy-done((bf16[6,32,256]{2,1,0:T(8,128)(2,1)S(1)}, bf16[6,32,256]{2,1,0:T(8,128)(2,1)}, u32[]{:S(2)}) %copy-start.1) | copy-done | bytes 98328
  2.3 0.0 copy-start.2
  2.3 0.7 %copy-done.2 = f32[6,256]{1,0:T(8,128)S(1)} copy-done((f32[6,256]{1,0:T(8,128)S(1)}, f32[6,256]{1,0:T(8,128)}, u32[]{:S(2)}) %copy-start.2) | copy-done | bytes 6168
  3.0 0.0 copy-start.3
  3.0 0.7 %copy-done.3 = f32[6,256]{1,0:T(8,128)S(1)} copy-done((f32[6,256]{1,0:T(8,128)S(1)}, f32[6,256]{1,0:T(8,128)}, u32[]{:S(2)}) %copy-start.3) | copy-done | bytes 6168
  3.7 0.0 copy-start.4
  3.7 0.7 %copy-done.4 = s32[16,16]{1,0:T(8,128)S(1)} copy-done((s32[16,16]{1,0:T(8,128)S(1)}, s32[16,16]{1,0:T(8,128)}, u32[]{:S(2)}) %copy-start.4) | copy-done | bytes 1048
  4.4 0.0 copy-start.5
  4.4 0.7 %copy-done.5 = s32[512]{0:T(512)S(1)} copy-done((s32[512]{0:T(512)S(1)}, s32[512]{0:T(512)}, u32[]{:S(2)}) %copy-start.5) | copy-done | bytes 2072
  5.1 0.0 copy-start.6
  5.1 0.7 %copy-done.6 = s32[32]{0:T(128)S(1)} copy-done((s32[32]{0:T(128)S(1)}, s32[32]{0:T(128)}, u32[]{:S(2)}) %copy-start.6) | copy-done | bytes 152
  5.7 29.7 %shard_map.73 = bf16[256,512]{1,0:T(8,128)(2,1)S(1)} custom-call(bf16[6,512,256]{2,1,0:T(8,128)(2,1)S(1)} %copy-done, bf16[6,32,256]{2,1,0:T(8,128)(2,1)S(1)} %copy-done.1, f32[6,256]{1,0:T(8,128)S(1)} %copy-done.2, f32[6,256]{1,0:T(8,128)S(1)} %copy-done.3, s32[1,512]{1,0:T(1,128)S(1)} %bitcast.4, s32[1,32]{1,0:T(1,128)S(1)} %bitcast.5, s32[16,16]{1,0:T(8,128)S(1)} %copy-done.4), custom_call_target="tpu_custom_call" | custom-call | tf_op jit(solution)/shard_map/pallas_call | solution.py:355
  35.4 0.7 %copy.9 = bf16[256,1,512]{2,0,1:T(8,128)(2,1)} copy(bf16[256,1,512]{2,0,1:T(8,128)(2,1)S(1)} %bitcast.3) | data formatting | bytes 524288
Async XLA Ops:
  0.0 1.4 %copy-start = (bf16[6,512,256]{2,1,0:T(8,128)(2,1)S(1)}, bf16[6,512,256]{2,1,0:T(8,128)(2,1)}, u32[]{:S(2)}) copy-start(bf16[6,512,256]{2,1,0:T(8,128)(2,1)} %train_hbm.1) | copy-start | bytes 4718596
  1.4 0.9 %copy-start.1 = (bf16[6,32,256]{2,1,0:T(8,128)(2,1)S(1)}, bf16[6,32,256]{2,1,0:T(8,128)(2,1)}, u32[]{:S(2)}) copy-start(bf16[6,32,256]{2,1,0:T(8,128)(2,1)} %val_hbm.1) | copy-start | bytes 294916
  2.3 0.7 %copy-start.2 = (f32[6,256]{1,0:T(8,128)S(1)}, f32[6,256]{1,0:T(8,128)}, u32[]{:S(2)}) copy-start(f32[6,256]{1,0:T(8,128)} %first_ref.1) | copy-start | bytes 18436
  3.0 0.7 %copy-start.3 = (f32[6,256]{1,0:T(8,128)S(1)}, f32[6,256]{1,0:T(8,128)}, u32[]{:S(2)}) copy-start(f32[6,256]{1,0:T(8,128)} %second_ref.1) | copy-start | bytes 18436
  3.7 0.7 %copy-start.4 = (s32[16,16]{1,0:T(8,128)S(1)}, s32[16,16]{1,0:T(8,128)}, u32[]{:S(2)}) copy-start(s32[16,16]{1,0:T(8,128)} %mask_ref.1) | copy-start | bytes 3076
  4.4 0.7 %copy-start.5 = (s32[512]{0:T(512)S(1)}, s32[512]{0:T(512)}, u32[]{:S(2)}) copy-start(s32[512]{0:T(512)} %param.11) | copy-start | bytes 6148
  5.1 0.7 %copy-start.6 = (s32[32]{0:T(128)S(1)}, s32[32]{0:T(128)}, u32[]{:S(2)}) copy-start(s32[32]{0:T(128)} %param.12) | copy-start | bytes 388

commit v2 on v1

--- a/solution.py
+++ b/solution.py
@@ -24,9 +24,9 @@
         return here
     below, above = here, extent - 1 - here
     least = jnp.minimum(below, above)
-    near = here - (step + 1) // 2 if step % 2 else here + step // 2
-    far = jnp.where(below < above, here + (step - least), here - (step - least))
-    return jnp.where(step <= 2 * least, near, far)
+    away = jnp.where(below < above, 1, -1)
+    near = here + away * ((step + 1) // 2 if step % 2 else -(step // 2))
+    return jnp.where(step <= 2 * least, near, here + away * (step - least))
 
 
 class Sends:
@@ -70,8 +70,9 @@
 
 def kernel(
     box, scale_factor,
-    train_hbm, val_hbm, first_ref, second_ref, tpair_ref, vpair_ref, mask_ref,
+    train_hbm, val_hbm, first_hbm, second_hbm, tpair_hbm, vpair_hbm, mask_hbm,
     out_ref,
+    first_ref, second_ref, tpair_ref, vpair_ref, mask_ref,
     gath, train, pre, tsq, tsq_in, part_out, part_in, own_part, vsq, vsq_in, labels,
     local_sems, send_sems, block_sems, pair_sems, label_sems,
 ):
@@ -96,6 +97,20 @@
     train_copy.start()
     val_copy = pltpu.make_async_copy(val_hbm, gath.at[me], local_sems.at[1])
     val_copy.start()
+    small_copies = [
+        pltpu.make_async_copy(src, dst, local_sems.at[3 + i])
+        for i, (src, dst) in enumerate(
+            (
+                (vpair_hbm, vpair_ref),
+                (first_hbm, first_ref),
+                (second_hbm, second_ref),
+                (tpair_hbm, tpair_ref),
+                (mask_hbm, mask_ref),
+            )
+        )
+    ]
+    for copy in small_copies:
+        copy.start()
 
     def neighbours(dim):
         here, extent = ((z, z_n), (y, y_n), (x, x_n))[dim]
@@ -221,8 +236,10 @@
                 grad = train[l, here, :].astype(jnp.float32)
                 first = first_ref[pl.ds(l, 1), :] * 0.9
                 second_m = second_ref[pl.ds(l, 1), :] * 0.999
-                root = lax.rsqrt(second_m + 0.001 * grad * grad)
-                value = (first + 0.1 * grad) * root / (1.0 + 1e-08 * root)
+                spread = second_m + 0.001 * grad * grad
+                root = lax.rsqrt(spread)
+                more = 1.0 + 1e-08 * root
+                value = (first + 0.1 * grad) * lax.rsqrt(spread * more * more)
                 total = total + value * value
                 pre[l, here, :] = value.astype(jnp.bfloat16)
             tsq[here, :] = jnp.broadcast_to(jnp.sum(total, axis=1, keepdims=True), (CHUNK, LANES))
@@ -300,40 +317,55 @@
             )
 
     column(0)
+    small_copies[0].wait()
     lane_block = lax.broadcasted_iota(jnp.int32, (1, LANES), 1) // val_dev
     own_labels = jnp.concatenate([vpair_ref[...]] * tile_blocks, axis=1)
     labels[me] = jnp.where(lane_block == me % tile_blocks, own_labels, -1)
     label_start(2)
     train_copy.wait()
-    precondition(0, tr_ex // 2)
-    label_line(2)
-    label_start(1)
-    second(0)
-    for step in range(1, z_n):
-        column(step)
-        if step == 1:
-            precondition(tr_ex // 2, tr_ex)
-            sends.go(tsq.at[theirs], tsq_in, local_sems.at[2], other_core)
-            label_line(1)
-            label_start(0)
-            second(step)
-            val_copy.wait()
-        else:
-            label_take(0, step - 1)
-            third(step - 2)
-            product(step - 2)
-            second(step)
-    pair_wait(tsq_in, local_sems.at[2])
-    if z_n > 1:
-        label_take(0, z_n - 1)
-        third(z_n - 2)
-        product(z_n - 2)
-    for step in range(z_n - 2):
-        finish(step)
-    third(z_n - 1)
-    product(z_n - 1)
-    for step in range(max(z_n - 2, 0), z_n):
-        finish(step)
+    for copy in small_copies[1:]:
+        copy.wait()
+
+    def last_quarter(start, stop):
+        precondition(start, stop)
+        sends.go(tsq.at[theirs], tsq_in, local_sems.at[2], other_core)
+
+    def label_mid(_):
+        label_line(2)
+        label_start(1)
+
+    def label_late(_):
+        label_line(1)
+        label_start(0)
+
+    def multiply(step):
+        third(step)
+        product(step)
+
+    quarter = tr_ex // 4
+    events = [
+        (0.5, lambda _: precondition(0, quarter), 0),
+        (1.9, label_mid, 0),
+        (2.5, lambda _: precondition(quarter, 2 * quarter), 0),
+        (2.9, label_late, 0),
+        (4.5, lambda _: precondition(2 * quarter, 3 * quarter), 0),
+        (5.0, lambda _: last_quarter(3 * quarter, tr_ex), 0),
+        (6.0, lambda _: val_copy.wait(), 0),
+    ]
+    for step in range(z_n):
+        if step:
+            events.append((2.0 * step - (0.0 if step < 2 else 0.5), column, step))
+            events.append((2.9 + 2.0 * step, lambda k: label_take(0, k), step))
+        events.append((3.0 * step + 1.7, second, step))
+        events.append((3.0 * step + 4.9 if step else 6.5, multiply, step))
+    for _, act, step in sorted(events, key=lambda event: event[0]):
+        act(step)
+        if act is multiply:
+            if step == 0:
+                pair_wait(tsq_in, local_sems.at[2])
+            else:
+                finish(step - 1)
+    finish(z_n - 1)
     sends.finish()
 
 
@@ -351,13 +383,18 @@
         plane_cols = y_n * x_n * val_dev
         scale_factor = float(lay_dev * layer_n * width) ** 0.25
         vmem = pl.BlockSpec(memory_space=pltpu.VMEM)
-        hbm = pl.BlockSpec(memory_space=pl.ANY)
+        hbm = pl.BlockSpec(memory_space=pltpu.HBM)
         scores = pl.pallas_call(
             functools.partial(kernel, box, scale_factor),
             out_shape=jax.ShapeDtypeStruct((rows, ex_n * val_dev), jnp.bfloat16),
-            in_specs=[hbm, hbm, vmem, vmem, vmem, vmem, vmem],
+            in_specs=[hbm] * 7,
             out_specs=vmem,
             scratch_shapes=[
+                pltpu.VMEM(first_moment.shape, jnp.float32),
+                pltpu.VMEM(second_moment.shape, jnp.float32),
+                pltpu.VMEM((1, tr_ex), jnp.int32),
+                pltpu.VMEM((1, val_dev), jnp.int32),
+                pltpu.VMEM(block_mask.shape, jnp.int32),
                 pltpu.VMEM((ex_n, lay_dev, val_dev, width), jnp.bfloat16),
                 pltpu.VMEM((lay_dev, tr_ex, width), jnp.bfloat16),
                 pltpu.VMEM((lay_dev, tr_ex, width), jnp.bfloat16),
@@ -369,14 +406,14 @@
                 pltpu.VMEM((z_n, 8, plane_cols), jnp.float32),
                 pltpu.VMEM((z_n, 8, plane_cols), jnp.float32),
                 pltpu.VMEM((ex_n, 1, LANES), jnp.int32),
-                pltpu.SemaphoreType.DMA((3,)),
+                pltpu.SemaphoreType.DMA((8,)),
                 pltpu.SemaphoreType.DMA((send_sites(box, z_n),)),
                 pltpu.SemaphoreType.DMA((2, ex_n)),
                 pltpu.SemaphoreType.DMA((2, z_n)),
                 pltpu.SemaphoreType.DMA((3, max(box))),
             ],
             compiler_params=pltpu.CompilerParams(
-                collective_id=0, has_side_effects=True, vmem_limit_bytes=48 * 1024 * 1024
+                collective_id=0, has_side_effects=True, vmem_limit_bytes=64 * 1024 * 1024
             ),
         )(
             train_sketch, val_sketch, first_moment, second_moment,

time: 36.5 us -> 31.1 us (0.85)
  local copies, waits for them, and re-layouts: 6.43 us -> 1.67 us
  Pallas kernels: 29.7 us -> 29.3 us
    unnamed x15 -> x1, local copies, waits for them, and re-layouts: 6.43 us -> 1.67 us
    pallas_call x1, Pallas kernels: 29.7 us -> 29.3 us  [local(): pl.pallas_call(functools.partial(kernel, box, scale_factor), out_shape=ja...]
where the time goes in v2:
time: 31.1 us; the launch traced here: 31 us
  Pallas kernels  29.3 us (94%)
  local copies, waits for them, and re-layouts  1.67 us (5%)
    pallas_call x1, Pallas kernels, local(): pl.pallas_call(functools.partial(kernel, box, scale_factor), out_shape=ja...  29.3 us
    unnamed x1, local copies, waits for them, and re-layouts  1.67 us

profile of v2, /device:TPU:0, one launch (start us, length us, event | category | flops | bytes accessed | tf_op | source)
XLA Modules:
  0.0 31.0 jit_solution(306445280694694045)
XLA Ops:
  0.0 29.3 %shard_map.73 = bf16[256,512]{1,0:T(8,128)(2,1)} custom-call(bf16[6,512,256]{2,1,0:T(8,128)(2,1)} %train_hbm.1, bf16[6,32,256]{2,1,0:T(8,128)(2,1)} %val_hbm.1, f32[6,256]{1,0:T(8,128)} %first_hbm.1, f32[6,256]{1,0:T(8,128)} %second_hbm.1, s32[1,512]{1,0:T(1,128)} %bitcast.4, s32[1,32]{1,0:T(1,128)} %bitcast.5, s32[16,16]{1,0:T(8,128)} %mask_hbm.1), custom_call_target="tpu_custom_call" | custom-call | tf_op jit(solution)/shard_map/pallas_call | solution.py:387
  29.3 1.7 %copy.9 = bf16[256,1,512]{2,0,1:T(8,128)(2,1)} copy(bf16[256,1,512]{2,0,1:T(8,128)(2,1)} %bitcast.3) | data formatting | bytes 524288

commit v3 on v2

--- a/solution.py
+++ b/solution.py
@@ -120,13 +120,15 @@
 
         if extent == 1:
             return []
+        if dim == 0:
+            return [(device(visit(here, extent, k)), None) for k in range(1, extent)]
         if extent == 2:
             return [(device(1 - here), None)]
         return [(device(here + 1), here < extent - 1), (device(here - 1), here > 0)]
 
     def onward(dim, came_from):
         here, extent = ((z, z_n), (y, y_n), (x, x_n))[dim]
-        if extent <= 2:
+        if extent <= 2 or dim == 0:
             return []
         pos = jnp.where(came_from < here, here + 1, here - 1)
         device = at_ex(*(pos if d == dim else c for d, c in enumerate((z, y, x))))
@@ -167,12 +169,17 @@
         for h in (0, 1):
             if step:
                 wait_block(h, where)
-                send_block(h, where, onward(0, plane))
-            else:
-                send_block(h, where, neighbours(0), True)
             send_block(h, where, neighbours(order[h][0]), not step)
+        if not step:
+            for target in neighbours(0)[:1]:
+                for h in (0, 1):
+                    send_block(h, where, [target], True)
         for h in (0, 1):
             send_block(h, where, neighbours(order[h][1]), not step)
+        if not step:
+            for target in neighbours(0)[1:]:
+                for h in (0, 1):
+                    send_block(h, where, [target], True)
 
     def second(step):
         plane = visit(z, z_n, step)
@@ -266,17 +273,7 @@
 
             part_out[step, :, cols] = dot(theirs).astype(jnp.bfloat16)
             if j == tiles - 1:
-                sends.go(part_out.at[step], part_in.at[step], pair_sems.at[0, step], other_core)
-            squares = None
-            for l in range(lay_dev):
-                value = layer(l).astype(jnp.float32)
-                squares = value * value if squares is None else squares + value * value
-            vsq[step, :, cols] = lax.dot_general(
-                jnp.ones((8, width), jnp.float32), squares, (((1,), (1,)), ((), ())),
-                precision=lax.Precision.HIGHEST, preferred_element_type=jnp.float32,
-            )
-            if j == tiles - 1:
-                sends.go(vsq.at[step], vsq_in.at[step], pair_sems.at[1, step], other_core)
+                sends.go(part_out.at[step], part_in.at[step], pair_sems.at[step], other_core)
             own_part[step, :, cols] = dot(mine)
 
     def pair_wait(buffer, sem):
@@ -293,23 +290,26 @@
         for j in range(tiles):
             first = plane * plane_blocks + j * tile_blocks
             row = labels[first]
+            total_sq = row[1:2]
+            row = row[0:1]
             for i in range(1, tile_blocks):
-                row = jnp.maximum(row, labels[first + i])
-            val_hot = (label_ids == row).astype(jnp.float32).astype(jnp.bfloat16)
+                more = labels[first + i]
+                row = jnp.maximum(row, more[0:1])
+                total_sq = total_sq + more[1:2]
+            val_hot = (label_ids == row.astype(jnp.int32)).astype(jnp.float32).astype(jnp.bfloat16)
             val_table = jnp.dot(table, val_hot, preferred_element_type=jnp.float32)
             weights.append(
                 row_scale
+                * lax.rsqrt(total_sq + 1e-06)
                 * lax.dot_general(
                     row_hot, val_table.astype(jnp.bfloat16), (((0,), (0,)), ((), ())),
                     preferred_element_type=jnp.float32,
                 )
             )
-        pair_wait(vsq_in.at[step], pair_sems.at[1, step])
-        pair_wait(part_in.at[step], pair_sems.at[0, step])
+        pair_wait(part_in.at[step], pair_sems.at[step])
         for j in range(tiles):
             cols = pl.ds(j * LANES, LANES)
-            total_sq = vsq[step, pl.ds(0, 1), cols] + vsq_in[step, pl.ds(0, 1), cols]
-            weight = weights[j] * lax.rsqrt(total_sq + 1e-06)
+            weight = weights[j]
             raw = own_part[step, :, cols] + part_in[step, :, cols].astype(jnp.float32)
             place = pl.multiple_of((plane * tiles + j) * LANES, LANES)
             out_ref[:, pl.ds(place, LANES)] = jnp.where(weight != 0.0, raw * weight, 0.0).astype(
@@ -317,13 +317,29 @@
             )
 
     column(0)
-    small_copies[0].wait()
+    val_copy.wait()
+    squares = None
+    for l in range(lay_dev):
+        value = gath[me, l].astype(jnp.float32)
+        squares = value * value if squares is None else squares + value * value
+    own_sq = lax.dot_general(
+        jnp.ones((8, width), jnp.float32), squares, (((1,), (1,)), ((), ())),
+        precision=lax.Precision.HIGHEST, preferred_element_type=jnp.float32,
+    )
     lane_block = lax.broadcasted_iota(jnp.int32, (1, LANES), 1) // val_dev
-    own_labels = jnp.concatenate([vpair_ref[...]] * tile_blocks, axis=1)
-    labels[me] = jnp.where(lane_block == me % tile_blocks, own_labels, -1)
-    label_start(2)
+    mine_here = lane_block == me % tile_blocks
+    vsq[...] = jnp.where(mine_here, jnp.concatenate([own_sq] * tile_blocks, axis=1), 0.0)
+    sends.go(vsq, vsq_in, local_sems.at[8], other_core)
+
+    def label_first(_):
+        pair_wait(vsq_in, local_sems.at[8])
+        own_labels = jnp.concatenate([vpair_ref[...]] * tile_blocks, axis=1)
+        labels[me, pl.ds(0, 1)] = jnp.where(mine_here, own_labels, -1).astype(jnp.float32)
+        labels[me, pl.ds(1, 1)] = vsq[pl.ds(0, 1), :] + vsq_in[pl.ds(0, 1), :]
+        label_start(2)
+
     train_copy.wait()
-    for copy in small_copies[1:]:
+    for copy in small_copies:
         copy.wait()
 
     def last_quarter(start, stop):
@@ -345,17 +361,17 @@
     quarter = tr_ex // 4
     events = [
         (0.5, lambda _: precondition(0, quarter), 0),
-        (1.9, label_mid, 0),
+        (1.6, label_first, 0),
+        (3.4, label_mid, 0),
         (2.5, lambda _: precondition(quarter, 2 * quarter), 0),
-        (2.9, label_late, 0),
+        (5.6, label_late, 0),
         (4.5, lambda _: precondition(2 * quarter, 3 * quarter), 0),
         (5.0, lambda _: last_quarter(3 * quarter, tr_ex), 0),
-        (6.0, lambda _: val_copy.wait(), 0),
     ]
     for step in range(z_n):
         if step:
             events.append((2.0 * step - (0.0 if step < 2 else 0.5), column, step))
-            events.append((2.9 + 2.0 * step, lambda k: label_take(0, k), step))
+            events.append((3.0 * step + 4.8, lambda k: label_take(0, k), step))
         events.append((3.0 * step + 1.7, second, step))
         events.append((3.0 * step + 4.9 if step else 6.5, multiply, step))
     for _, act, step in sorted(events, key=lambda event: event[0]):
@@ -403,21 +419,26 @@
                 pltpu.VMEM((z_n, rows, plane_cols), jnp.bfloat16),
                 pltpu.VMEM((z_n, rows, plane_cols), jnp.bfloat16),
                 pltpu.VMEM((z_n, rows, plane_cols), jnp.float32),
-                pltpu.VMEM((z_n, 8, plane_cols), jnp.float32),
-                pltpu.VMEM((z_n, 8, plane_cols), jnp.float32),
-                pltpu.VMEM((ex_n, 1, LANES), jnp.int32),
-                pltpu.SemaphoreType.DMA((8,)),
+                pltpu.VMEM((8, LANES), jnp.float32),
+                pltpu.VMEM((8, LANES), jnp.float32),
+                pltpu.VMEM((ex_n, 2, LANES), jnp.float32),
+                pltpu.SemaphoreType.DMA((9,)),
                 pltpu.SemaphoreType.DMA((send_sites(box, z_n),)),
                 pltpu.SemaphoreType.DMA((2, ex_n)),
-                pltpu.SemaphoreType.DMA((2, z_n)),
+                pltpu.SemaphoreType.DMA((z_n,)),
                 pltpu.SemaphoreType.DMA((3, max(box))),
             ],
             compiler_params=pltpu.CompilerParams(
-                collective_id=0, has_side_effects=True, vmem_limit_bytes=64 * 1024 * 1024
+                collective_id=0, has_side_effects=True, vmem_limit_bytes=48 * 1024 * 1024
             ),
         )(
-            train_sketch, val_sketch, first_moment, second_moment,
-            train_pair[None, :], val_pair[None, :], block_mask,
+            *(
+                pltpu.with_memory_space_constraint(array, pltpu.HBM)
+                for array in (
+                    train_sketch, val_sketch, first_moment, second_moment,
+                    train_pair[None, :], val_pair[None, :], block_mask,
+                )
+            )
         )
         return scores[:, None, :]
 

time: 31.1 us -> 28.9 us (0.929)
  Pallas kernels: 29.3 us -> 28 us
  local copies, waits for them, and re-layouts: 1.67 us -> 0.71 us
    pallas_call x1, Pallas kernels: 29.3 us -> 28 us  [local(): pl.pallas_call(functools.partial(kernel, box, scale_factor), out_shape=ja...]
    unnamed x1, local copies, waits for them, and re-layouts: 1.67 us -> 0.71 us
where the time goes in v3:
time: 28.9 us; the launch traced here: 28.7 us
  Pallas kernels  28 us (97%)
  local copies, waits for them, and re-layouts  0.71 us (2%)
    pallas_call x1, Pallas kernels, local(): pl.pallas_call(functools.partial(kernel, box, scale_factor), out_shape=ja...  28 us
    unnamed x1, local copies, waits for them, and re-layouts  0.71 us

profile of v3, /device:TPU:0, one launch (start us, length us, event | category | flops | bytes accessed | tf_op | source)
XLA Modules:
  0.0 28.7 jit_solution(18260245040234033580)
XLA Ops:
  0.0 28.0 %shard_map.73 = bf16[256,512]{1,0:T(8,128)(2,1)S(1)} custom-call(bf16[6,512,256]{2,1,0:T(8,128)(2,1)} %train_hbm.1, bf16[6,32,256]{2,1,0:T(8,128)(2,1)} %val_hbm.1, f32[6,256]{1,0:T(8,128)} %first_hbm.1, f32[6,256]{1,0:T(8,128)} %second_hbm.1, s32[1,512]{1,0:T(1,128)} %bitcast.4, s32[1,32]{1,0:T(1,128)} %bitcast.5, s32[16,16]{1,0:T(8,128)} %mask_hbm.1), custom_call_target="tpu_custom_call" | custom-call | tf_op jit(solution)/shard_map/pallas_call | solution.py:403
  28.0 0.7 %copy.9 = bf16[256,1,512]{2,0,1:T(8,128)(2,1)} copy(bf16[256,1,512]{2,0,1:T(8,128)(2,1)S(1)} %bitcast.3) | data formatting | bytes 524288

commit v4 on v3

--- a/solution.py
+++ b/solution.py
@@ -65,7 +65,7 @@
     z_n, y_n, x_n = box
     line = lambda n: 0 if n == 1 else 1 if n == 2 else 2 + (n - 1)
     per = 2 + 2 * (line(y_n) + line(x_n) + y_n * line(x_n) + x_n * line(y_n))
-    return z_n * (per + 4) + 16 + 2 * z_n + 3 * (z_n + y_n + x_n)
+    return z_n * (per + 4) + 32 + 2 * z_n + 3 * (z_n + y_n + x_n)
 
 
 def kernel(
@@ -120,15 +120,13 @@
 
         if extent == 1:
             return []
-        if dim == 0:
-            return [(device(visit(here, extent, k)), None) for k in range(1, extent)]
         if extent == 2:
             return [(device(1 - here), None)]
         return [(device(here + 1), here < extent - 1), (device(here - 1), here > 0)]
 
     def onward(dim, came_from):
         here, extent = ((z, z_n), (y, y_n), (x, x_n))[dim]
-        if extent <= 2 or dim == 0:
+        if extent <= 2:
             return []
         pos = jnp.where(came_from < here, here + 1, here - 1)
         device = at_ex(*(pos if d == dim else c for d, c in enumerate((z, y, x))))
@@ -162,6 +160,9 @@
         pltpu.make_async_copy(block(h, where), block(h, where), block_sems.at[h, where]).wait()
 
     order = ((1, 2), (2, 1))
+    relays = box == (4, 2, 2)
+    at_end = jnp.logical_or(z == 0, z == z_n - 1)
+    in_middle = jnp.logical_and(z > 0, z < z_n - 1)
 
     def column(step):
         plane = visit(z, z_n, step)
@@ -169,17 +170,12 @@
         for h in (0, 1):
             if step:
                 wait_block(h, where)
+                send_block(h, where, onward(0, plane))
+            else:
+                send_block(h, where, neighbours(0), True)
             send_block(h, where, neighbours(order[h][0]), not step)
-        if not step:
-            for target in neighbours(0)[:1]:
-                for h in (0, 1):
-                    send_block(h, where, [target], True)
         for h in (0, 1):
             send_block(h, where, neighbours(order[h][1]), not step)
-        if not step:
-            for target in neighbours(0)[1:]:
-                for h in (0, 1):
-                    send_block(h, where, [target], True)
 
     def second(step):
         plane = visit(z, z_n, step)
@@ -191,10 +187,34 @@
                 where = slot(plane, pos, x) if dim == 1 else slot(plane, y, pos)
                 wait_block(h, where)
                 send_block(h, where, onward(dim, pos))
-                send_block(h, where, neighbours(last))
+                if not relays:
+                    send_block(h, where, neighbours(last))
+                elif step != 2:
+                    cond = (None, in_middle, None, at_end)[step]
+                    send_block(h, where, [(device, cond) for device, _ in neighbours(last)])
+
+    def relay(step):
+        where = slot(visit(z, z_n, step), 1 - y, 1 - x)
+        pair = z + 1 - 2 * (z % 2)
+        target = at_ex(z_n - 1 - z if step == 2 else pair, y, x)
+        cond = in_middle if step else None
+        for h in (0, 1):
+            if step == 2:
+                pl.when(in_middle)(lambda h=h: wait_block(h, where))
+            else:
+                wait_block(h, where)
+            if step < 3:
+                send_block(h, where, [(target, cond)])
 
     def third(step):
         plane = visit(z, z_n, step)
+        if relays:
+            for h in (0, 1):
+                wait_block(h, slot(plane, y, 1 - x) if h == 0 else slot(plane, 1 - y, x))
+                if step == 2:
+                    where = slot(plane, 1 - y, 1 - x)
+                    pl.when(at_end)(lambda h=h, where=where: wait_block(h, where))
+            return
         for h in (0, 1):
             dim, last = order[h]
             here, extent = ((z, z_n), (y, y_n), (x, x_n))[dim]
@@ -362,18 +382,21 @@
     events = [
         (0.5, lambda _: precondition(0, quarter), 0),
         (1.6, label_first, 0),
-        (3.4, label_mid, 0),
-        (2.5, lambda _: precondition(quarter, 2 * quarter), 0),
+        (3.4, lambda _: precondition(quarter, 2 * quarter), 0),
+        (3.5, lambda _: precondition(2 * quarter, 3 * quarter), 0),
+        (3.6, label_mid, 0),
+        (4.5, lambda _: last_quarter(3 * quarter, tr_ex), 0),
         (5.6, label_late, 0),
-        (4.5, lambda _: precondition(2 * quarter, 3 * quarter), 0),
-        (5.0, lambda _: last_quarter(3 * quarter, tr_ex), 0),
     ]
     for step in range(z_n):
         if step:
-            events.append((2.0 * step - (0.0 if step < 2 else 0.5), column, step))
-            events.append((3.0 * step + 4.8, lambda k: label_take(0, k), step))
-        events.append((3.0 * step + 1.7, second, step))
-        events.append((3.0 * step + 4.9 if step else 6.5, multiply, step))
+            events.append((1.0 + 2.0 * step if step > 1 else 2.9, column, step))
+            events.append((7.2 + 1.6 * (step - 1), lambda k: label_take(0, k), step))
+        events.append((2.2 + 4.5 * step if step < 2 else 8.5 + step, second, step))
+        events.append((7.5 + 2.2 * step if step < 2 else 2.4 * step + 8.1, multiply, step))
+    if relays:
+        for key, step in ((4.9, 0), (9.0, 1), (10.0, 2), (15.0, 3)):
+            events.append((key, relay, step))
     for _, act, step in sorted(events, key=lambda event: event[0]):
         act(step)
         if act is multiply:

time: 28.9 us -> 29.1 us (level)
  Pallas kernels: 28 us -> 28.3 us
where the time goes in v4:
time: 29.1 us; the launch traced here: 29 us
  Pallas kernels  28.3 us (97%)
  local copies, waits for them, and re-layouts  0.71 us (2%)
    pallas_call x1, Pallas kernels, local(): pl.pallas_call(functools.partial(kernel, box, scale_factor), out_shape=ja...  28.3 us
    unnamed x1, local copies, waits for them, and re-layouts  0.71 us

profile of v4, /device:TPU:0, one launch (start us, length us, event | category | flops | bytes accessed | tf_op | source)
XLA Modules:
  0.0 29.0 jit_solution(9292831481180515689)
XLA Ops:
  0.0 28.3 %shard_map.73 = bf16[256,512]{1,0:T(8,128)(2,1)S(1)} custom-call(bf16[6,512,256]{2,1,0:T(8,128)(2,1)} %train_hbm.1, bf16[6,32,256]{2,1,0:T(8,128)(2,1)} %val_hbm.1, f32[6,256]{1,0:T(8,128)} %first_hbm.1, f32[6,256]{1,0:T(8,128)} %second_hbm.1, s32[1,512]{1,0:T(1,128)} %bitcast.4, s32[1,32]{1,0:T(1,128)} %bitcast.5, s32[16,16]{1,0:T(8,128)} %mask_hbm.1), custom_call_target="tpu_custom_call" | custom-call | tf_op jit(solution)/shard_map/pallas_call | solution.py:426
  28.3 0.7 %copy.9 = bf16[256,1,512]{2,0,1:T(8,128)(2,1)} copy(bf16[256,1,512]{2,0,1:T(8,128)(2,1)S(1)} %bitcast.3) | data formatting | bytes 524288

commit v5 on v4

--- a/solution.py
+++ b/solution.py
@@ -132,6 +132,10 @@
         device = at_ex(*(pos if d == dim else c for d, c in enumerate((z, y, x))))
         return [(device, jnp.logical_and(pos >= 0, pos < extent))]
 
+    relays = box == (4, 2, 2)
+    at_end = jnp.logical_or(z == 0, z == z_n - 1)
+    in_middle = jnp.logical_and(z > 0, z < z_n - 1)
+
     barrier = pltpu.get_barrier_semaphore()
     pl.semaphore_signal(barrier, inc=1, device_id=other_core, device_id_type=MESH)
     expected = 1
@@ -146,6 +150,14 @@
             else:
                 pl.when(cond)(greet)
                 expected = expected + jnp.where(cond, 1, 0)
+    if relays:
+        @pl.when(at_end)
+        def _():
+            pl.semaphore_signal(
+                barrier, inc=1, device_id=at_ex(z_n - 1 - z, y, x), device_id_type=MESH
+            )
+
+        expected = expected + jnp.where(at_end, 1, 0)
     pl.semaphore_wait(barrier, expected)
 
     def block(h, where):
@@ -160,9 +172,6 @@
         pltpu.make_async_copy(block(h, where), block(h, where), block_sems.at[h, where]).wait()
 
     order = ((1, 2), (2, 1))
-    relays = box == (4, 2, 2)
-    at_end = jnp.logical_or(z == 0, z == z_n - 1)
-    in_middle = jnp.logical_and(z > 0, z < z_n - 1)
 
     def column(step):
         plane = visit(z, z_n, step)
@@ -170,12 +179,16 @@
         for h in (0, 1):
             if step:
                 wait_block(h, where)
-                send_block(h, where, onward(0, plane))
+                if not (relays and step == z_n - 1):
+                    send_block(h, where, onward(0, plane))
             else:
                 send_block(h, where, neighbours(0), True)
             send_block(h, where, neighbours(order[h][0]), not step)
         for h in (0, 1):
             send_block(h, where, neighbours(order[h][1]), not step)
+        if relays and not step:
+            for h in (0, 1):
+                send_block(h, where, [(at_ex(z_n - 1 - z, y, x), at_end)], True)
 
     def second(step):
         plane = visit(z, z_n, step)

time: 29.1 us -> 29.6 us (1.017)
  Pallas kernels: 28.3 us -> 28.7 us
    pallas_call x1, Pallas kernels: 28.3 us -> 28.7 us  [local(): pl.pallas_call(functools.partial(kernel, box, scale_factor), out_shape=ja...]
where the time goes in v5:
time: 29.6 us; the launch traced here: 29.5 us
  Pallas kernels  28.7 us (97%)
  local copies, waits for them, and re-layouts  0.71 us (2%)
    pallas_call x1, Pallas kernels, local(): pl.pallas_call(functools.partial(kernel, box, scale_factor), out_shape=ja...  28.7 us
    unnamed x1, local copies, waits for them, and re-layouts  0.71 us

profile of v5, /device:TPU:0, one launch (start us, length us, event | category | flops | bytes accessed | tf_op | source)
XLA Modules:
  0.0 29.5 jit_solution(15364555544385988660)
XLA Ops:
  0.0 28.7 %shard_map.73 = bf16[256,512]{1,0:T(8,128)(2,1)S(1)} custom-call(bf16[6,512,256]{2,1,0:T(8,128)(2,1)} %train_hbm.1, bf16[6,32,256]{2,1,0:T(8,128)(2,1)} %val_hbm.1, f32[6,256]{1,0:T(8,128)} %first_hbm.1, f32[6,256]{1,0:T(8,128)} %second_hbm.1, s32[1,512]{1,0:T(1,128)} %bitcast.4, s32[1,32]{1,0:T(1,128)} %bitcast.5, s32[16,16]{1,0:T(8,128)} %mask_hbm.1), custom_call_target="tpu_custom_call" | custom-call | tf_op jit(solution)/shard_map/pallas_call | solution.py:439
  28.8 0.7 %copy.9 = bf16[256,1,512]{2,0,1:T(8,128)(2,1)} copy(bf16[256,1,512]{2,0,1:T(8,128)(2,1)S(1)} %bitcast.3) | data formatting | bytes 524288

commit v6 on v4

--- a/solution.py
+++ b/solution.py
@@ -65,7 +65,7 @@
     z_n, y_n, x_n = box
     line = lambda n: 0 if n == 1 else 1 if n == 2 else 2 + (n - 1)
     per = 2 + 2 * (line(y_n) + line(x_n) + y_n * line(x_n) + x_n * line(y_n))
-    return z_n * (per + 4) + 32 + 2 * z_n + 3 * (z_n + y_n + x_n)
+    return z_n * (per + 4) + 64 + 2 * z_n + 3 * (z_n + y_n + x_n)
 
 
 def kernel(
@@ -164,18 +164,27 @@
     at_end = jnp.logical_or(z == 0, z == z_n - 1)
     in_middle = jnp.logical_and(z > 0, z < z_n - 1)
 
-    def column(step):
+    def under(cond, targets):
+        if cond is None:
+            return targets
+        return [(d, cond if c is None else jnp.logical_and(c, cond)) for d, c in targets]
+
+    def column(step, cond=None):
         plane = visit(z, z_n, step)
         where = slot(plane, y, x)
         for h in (0, 1):
-            if step:
+            if not step:
+                send_block(h, where, neighbours(0), True)
+            elif cond is None:
                 wait_block(h, where)
                 send_block(h, where, onward(0, plane))
             else:
-                send_block(h, where, neighbours(0), True)
-            send_block(h, where, neighbours(order[h][0]), not step)
+                pl.when(cond)(lambda h=h: wait_block(h, where))
+                if cond is in_middle:
+                    send_block(h, where, under(cond, onward(0, plane)))
+            send_block(h, where, under(cond, neighbours(order[h][0])), not step)
         for h in (0, 1):
-            send_block(h, where, neighbours(order[h][1]), not step)
+            send_block(h, where, under(cond, neighbours(order[h][1])), not step)
 
     def second(step):
         plane = visit(z, z_n, step)
@@ -189,21 +198,20 @@
                 send_block(h, where, onward(dim, pos))
                 if not relays:
                     send_block(h, where, neighbours(last))
-                elif step != 2:
-                    cond = (None, in_middle, None, at_end)[step]
-                    send_block(h, where, [(device, cond) for device, _ in neighbours(last)])
+                else:
+                    send_block(h, where, under(at_end if step > 1 else None, neighbours(last)))
 
     def relay(step):
         where = slot(visit(z, z_n, step), 1 - y, 1 - x)
         pair = z + 1 - 2 * (z % 2)
         target = at_ex(z_n - 1 - z if step == 2 else pair, y, x)
-        cond = in_middle if step else None
+        cond = in_middle if step else at_end
         for h in (0, 1):
             if step == 2:
                 pl.when(in_middle)(lambda h=h: wait_block(h, where))
             else:
                 wait_block(h, where)
-            if step < 3:
+            if step in (0, 2):
                 send_block(h, where, [(target, cond)])
 
     def third(step):
@@ -390,12 +398,17 @@
     ]
     for step in range(z_n):
         if step:
-            events.append((1.0 + 2.0 * step if step > 1 else 2.9, column, step))
+            if relays and step > 1:
+                early, late = ((3.0, 6.8), (7.0, 10.6))[step - 2]
+                events.append((early, lambda k: column(k, in_middle), step))
+                events.append((late, lambda k: column(k, at_end), step))
+            else:
+                events.append((1.0 + 2.0 * step if step > 1 else 2.9, column, step))
             events.append((7.2 + 1.6 * (step - 1), lambda k: label_take(0, k), step))
         events.append((2.2 + 4.5 * step if step < 2 else 8.5 + step, second, step))
         events.append((7.5 + 2.2 * step if step < 2 else 2.4 * step + 8.1, multiply, step))
     if relays:
-        for key, step in ((4.9, 0), (9.0, 1), (10.0, 2), (15.0, 3)):
+        for key, step in ((4.9, 0), (9.6, 1), (10.0, 2), (15.0, 3)):
             events.append((key, relay, step))
     for _, act, step in sorted(events, key=lambda event: event[0]):
         act(step)

time: 29.1 us -> 34.3 us (1.18)
  Pallas kernels: 28.3 us -> 33.4 us
    pallas_call x1, Pallas kernels: 28.3 us -> 33.4 us  [local(): pl.pallas_call(functools.partial(kernel, box, scale_factor), out_shape=ja...]
where the time goes in v6:
time: 34.3 us; the launch traced here: 34.1 us
  Pallas kernels  33.4 us (97%)
  local copies, waits for them, and re-layouts  0.71 us (2%)
    pallas_call x1, Pallas kernels, local(): pl.pallas_call(functools.partial(kernel, box, scale_factor), out_shape=ja...  33.4 us
    unnamed x1, local copies, waits for them, and re-layouts  0.71 us

profile of v6, /device:TPU:0, one launch (start us, length us, event | category | flops | bytes accessed | tf_op | source)
XLA Modules:
  0.0 34.1 jit_solution(13149981475451945877)
XLA Ops:
  0.0 33.4 %shard_map.73 = bf16[256,512]{1,0:T(8,128)(2,1)S(1)} custom-call(bf16[6,512,256]{2,1,0:T(8,128)(2,1)} %train_hbm.1, bf16[6,32,256]{2,1,0:T(8,128)(2,1)} %val_hbm.1, f32[6,256]{1,0:T(8,128)} %first_hbm.1, f32[6,256]{1,0:T(8,128)} %second_hbm.1, s32[1,512]{1,0:T(1,128)} %bitcast.4, s32[1,32]{1,0:T(1,128)} %bitcast.5, s32[16,16]{1,0:T(8,128)} %mask_hbm.1), custom_call_target="tpu_custom_call" | custom-call | tf_op jit(solution)/shard_map/pallas_call | solution.py:439
  33.4 0.7 %copy.9 = bf16[256,1,512]{2,0,1:T(8,128)(2,1)} copy(bf16[256,1,512]{2,0,1:T(8,128)(2,1)S(1)} %bitcast.3) | data formatting | bytes 524288

commit v7 on v5

--- a/solution.py
+++ b/solution.py
@@ -403,7 +403,7 @@
     ]
     for step in range(z_n):
         if step:
-            events.append((1.0 + 2.0 * step if step > 1 else 2.9, column, step))
+            events.append((2.2 * step - 1.3 if step > 1 else 2.9, column, step))
             events.append((7.2 + 1.6 * (step - 1), lambda k: label_take(0, k), step))
         events.append((2.2 + 4.5 * step if step < 2 else 8.5 + step, second, step))
         events.append((7.5 + 2.2 * step if step < 2 else 2.4 * step + 8.1, multiply, step))

time: 29.6 us -> 32.9 us (1.11)
  Pallas kernels: 28.7 us -> 32 us
    pallas_call x1, Pallas kernels: 28.7 us -> 32 us  [local(): pl.pallas_call(functools.partial(kernel, box, scale_factor), out_shape=ja...]
where the time goes in v7:
time: 32.9 us; the launch traced here: 32.7 us
  Pallas kernels  32 us (97%)
  local copies, waits for them, and re-layouts  0.71 us (2%)
    pallas_call x1, Pallas kernels, local(): pl.pallas_call(functools.partial(kernel, box, scale_factor), out_shape=ja...  32 us
    unnamed x1, local copies, waits for them, and re-layouts  0.71 us

profile of v7, /device:TPU:0, one launch (start us, length us, event | category | flops | bytes accessed | tf_op | source)
XLA Modules:
  0.0 32.7 jit_solution(10945229685704759856)
XLA Ops:
  0.0 32.0 %shard_map.73 = bf16[256,512]{1,0:T(8,128)(2,1)S(1)} custom-call(bf16[6,512,256]{2,1,0:T(8,128)(2,1)} %train_hbm.1, bf16[6,32,256]{2,1,0:T(8,128)(2,1)} %val_hbm.1, f32[6,256]{1,0:T(8,128)} %first_hbm.1, f32[6,256]{1,0:T(8,128)} %second_hbm.1, s32[1,512]{1,0:T(1,128)} %bitcast.4, s32[1,32]{1,0:T(1,128)} %bitcast.5, s32[16,16]{1,0:T(8,128)} %mask_hbm.1), custom_call_target="tpu_custom_call" | custom-call | tf_op jit(solution)/shard_map/pallas_call | solution.py:439
  32.0 0.7 %copy.9 = bf16[256,1,512]{2,0,1:T(8,128)(2,1)} copy(bf16[256,1,512]{2,0,1:T(8,128)(2,1)S(1)} %bitcast.3) | data formatting | bytes 524288

commit v8 on v3

--- a/solution.py
+++ b/solution.py
@@ -373,7 +373,7 @@
             events.append((2.0 * step - (0.0 if step < 2 else 0.5), column, step))
             events.append((3.0 * step + 4.8, lambda k: label_take(0, k), step))
         events.append((3.0 * step + 1.7, second, step))
-        events.append((3.0 * step + 4.9 if step else 6.5, multiply, step))
+        events.append((3.0 * step + 4.9 if step else 7.75, multiply, step))
     for _, act, step in sorted(events, key=lambda event: event[0]):
         act(step)
         if act is multiply:

time: 28.9 us -> 29.1 us (level)
  Pallas kernels: 28 us -> 28.3 us
where the time goes in v8:
time: 29.1 us; the launch traced here: 29 us
  Pallas kernels  28.3 us (97%)
  local copies, waits for them, and re-layouts  0.71 us (2%)
    pallas_call x1, Pallas kernels, local(): pl.pallas_call(functools.partial(kernel, box, scale_factor), out_shape=ja...  28.3 us
    unnamed x1, local copies, waits for them, and re-layouts  0.71 us

profile of v8, /device:TPU:0, one launch (start us, length us, event | category | flops | bytes accessed | tf_op | source)
XLA Modules:
  0.0 29.0 jit_solution(12450119172035361566)
XLA Ops:
  0.0 28.3 %shard_map.73 = bf16[256,512]{1,0:T(8,128)(2,1)S(1)} custom-call(bf16[6,512,256]{2,1,0:T(8,128)(2,1)} %train_hbm.1, bf16[6,32,256]{2,1,0:T(8,128)(2,1)} %val_hbm.1, f32[6,256]{1,0:T(8,128)} %first_hbm.1, f32[6,256]{1,0:T(8,128)} %second_hbm.1, s32[1,512]{1,0:T(1,128)} %bitcast.4, s32[1,32]{1,0:T(1,128)} %bitcast.5, s32[16,16]{1,0:T(8,128)} %mask_hbm.1), custom_call_target="tpu_custom_call" | custom-call | tf_op jit(solution)/shard_map/pallas_call | solution.py:403
  28.3 0.7 %copy.9 = bf16[256,1,512]{2,0,1:T(8,128)(2,1)} copy(bf16[256,1,512]{2,0,1:T(8,128)(2,1)S(1)} %bitcast.3) | data formatting | bytes 524288
